TPU v7x, 512 devices: a whole 4x8x8 slice. The times are simulated.
512 devices in a mesh: dp: 32 (over z, y_hi), fsdp: 16 (over x, y_lo, core).
Axes of the slice: x: 4, y: 8 (y_hi: 4, y_lo: 2; y = y_hi * 2 + y_lo), z: 8, core: 2. Of those that a mesh axis runs over, the one named last changes fastest.
Arguments:
- tokens: bfloat16 [12288, 4096], P('dp', 'fsdp'), may hold values from -6 to 6
- gate_logits: bfloat16 [12288, 14336], P('dp', 'fsdp'), may hold values from -8 to 8
- linear_values: bfloat16 [12288, 14336], P('dp', 'fsdp'), may hold values from -6 to 6
- hidden_grad: bfloat16 [12288, 14336], P('dp', 'fsdp'), may hold values from -3 to 3
- basis: bfloat16 [4096, 512], P('fsdp'), may hold values from -0.09375 to 0.09375
- gate_moment: float32 [512, 14336], P('dp', 'fsdp'), may hold values from -0.75 to 0.75
- gate_second: float32 [512, 14336], P('dp', 'fsdp'), may hold values from 0.05 to 1
- linear_moment: float32 [512, 14336], P('dp', 'fsdp'), may hold values from -0.75 to 0.75
- linear_second: float32 [512, 14336], P('dp', 'fsdp'), may hold values from 0.05 to 1
Outputs:
- gate_update: float32 [4096, 14336], P('dp', 'fsdp')
- linear_update: float32 [4096, 14336], P('dp', 'fsdp')
- moment_gate: float32 [512, 14336], P('dp', 'fsdp')
- second_gate: float32 [512, 14336], P('dp', 'fsdp')
- moment_linear: float32 [512, 14336], P('dp', 'fsdp')
- second_linear: float32 [512, 14336], P('dp', 'fsdp')
All inputs are finite; a program needn't handle non-finite values.
Results may differ from a plain program's by a relative error of at most 0.0057.
Values may be sent and summed in bfloat16 or wider, within the bound.
A program may use at most 64 MiB of HBM per device.

v0:
```python
import jax
import jax.numpy as jnp
from jax import lax
from jax.sharding import PartitionSpec as P


def spread(value, axis, source):
    kept = jnp.where(lax.axis_index(axis) == source, value, 0).astype(value.dtype)
    return lax.psum(kept, axis)


def gradients(gate_logits, linear_values, hidden_grad):
    logits = gate_logits.astype(jnp.float32)
    values = linear_values.astype(jnp.float32)
    incoming = hidden_grad.astype(jnp.float32)
    sigmoid_gate = jax.nn.sigmoid(logits)
    activated = logits * sigmoid_gate
    gate_grad = (incoming * values * sigmoid_gate * (1.0 + logits * (1.0 - sigmoid_gate))).astype(
        jnp.bfloat16
    )
    linear_grad = (incoming * activated).astype(jnp.bfloat16)
    return (gate_grad, linear_grad)


def adam_step(moment, second, grad):
    moment_out = 0.9 * moment + 0.1 * grad
    second_out = 0.999 * second + 0.001 * grad * grad
    normalized = (moment_out / (jnp.sqrt(second_out) + 1e-08)).astype(jnp.bfloat16)
    return (moment_out, second_out, normalized)


def per_device(
    tokens,
    gate_logits,
    linear_values,
    hidden_grad,
    basis,
    gate_moment,
    gate_second,
    linear_moment,
    linear_second,
):
    block_rows = basis.shape[0]
    width = gate_logits.shape[1]
    rows_dp = block_rows * lax.axis_size("fsdp") // lax.axis_size("dp")
    features = lax.all_gather(tokens, "fsdp", axis=1, tiled=True)
    summed_proj = jnp.dot(
        features,
        lax.all_gather(basis, "fsdp", axis=0, tiled=True),
        preferred_element_type=jnp.float32,
    )
    projected = summed_proj.astype(jnp.bfloat16)
    gate_grad, linear_grad = gradients(gate_logits, linear_values, hidden_grad)
    first_row = lax.axis_index("dp") * rows_dp
    holder = first_row // block_rows
    block = spread(basis, "fsdp", holder)
    local_rows = lax.dynamic_slice_in_dim(block, first_row % block_rows, rows_dp, 0)

    def expand_one(piece):
        return jnp.dot(local_rows, piece, preferred_element_type=jnp.float32)

    both = jnp.concatenate([gate_grad, linear_grad], axis=1)
    subspace = lax.psum_scatter(
        lax.dot_general(
            projected, both, (((0,), (0,)), ((), ())), preferred_element_type=jnp.float32
        ),
        "dp",
        scatter_dimension=0,
        tiled=True,
    )
    moment_gate, second_gate, gate_norm = adam_step(gate_moment, gate_second, subspace[:, :width])
    moment_linear, second_linear, linear_norm = adam_step(
        linear_moment, linear_second, subspace[:, width:]
    )
    gate_update = expand_one(lax.all_gather(gate_norm, "dp", axis=0, tiled=True))
    linear_update = expand_one(lax.all_gather(linear_norm, "dp", axis=0, tiled=True))
    return (gate_update, linear_update, moment_gate, second_gate, moment_linear, second_linear)


def solution(mesh):
    placed = (
        P("dp", "fsdp"),
        P("dp", "fsdp"),
        P("dp", "fsdp"),
        P("dp", "fsdp"),
        P("fsdp", None),
        P("dp", "fsdp"),
        P("dp", "fsdp"),
        P("dp", "fsdp"),
        P("dp", "fsdp"),
    )
    return jax.shard_map(
        per_device,
        mesh=mesh,
        in_specs=placed,
        out_specs=(
            P("dp", "fsdp"),
            P("dp", "fsdp"),
            P("dp", "fsdp"),
            P("dp", "fsdp"),
            P("dp", "fsdp"),
            P("dp", "fsdp"),
        ),
        check_vma=False,
    )
```

profile of v0, /device:TPU:16, one launch (start us, length us, event | category | flops | bytes accessed | tf_op | source)
XLA Modules:
  0.0 524.1 jit_solution(9659957795164064031)
XLA Ops:
  7.2 0.0 all-gather.3.cloned.1.call-start
  7.2 0.7 all-gather.3.cloned.1.call-update
  7.9 0.0 all-gather.5.cloned.1.call-start
  7.9 0.7 all-gather.5.cloned.1.call-update
  8.7 0.0 reduce-scatter.2.cloned.1.call-start
  8.7 2.3 fusion.2
  11.0 50.0 %all-gather.3.cloned.1.call-done = bf16[384,4096]{1,0:T(8,128)(2,1)} async-done(((bf16[384,256]{1,0:T(8,128)(2,1)}), bf16[384,4096]{1,0:T(8,128)(2,1)}) %all-gather.3.cloned.1.call-update) | async-done | bytes 3145744 | tf_op jit(solution)/shard_map/all_gather | solution.py:46
  61.0 45.0 %all-gather.5.cloned.1.call-done = bf16[4096,512]{1,0:T(8,128)(2,1)} async-done(((bf16[256,512]{1,0:T(8,128)(2,1)}), bf16[4096,512]{1,0:T(8,128)(2,1)}) %all-gather.5.cloned.1.call-update) | async-done | bytes 4194320 | tf_op jit(solution)/shard_map/all_gather | solution.py:49
  106.0 7.8 %fusion.8 = f32[512,1792]{1,0:T(8,128)} fusion(bf16[384,896]{1,0:T(8,128)(2,1)S(1)} %get-tuple-element.13, bf16[384,896]{1,0:T(8,128)(2,1)S(1)} %get-tuple-element.12, bf16[384,4096]{1,0:T(8,128)(2,1)} %all-gather.3.cloned.1.call-done, bf16[4096,512]{1,0:T(8,128)(2,1)} %all-gather.5.cloned.1.call-done), kind=kOutput, calls=%fused_computation.13 | convolution fusion | flops 2318204928 | bytes 12386304 | tf_op jit(solution)/shard_map/dot_general | solution.py:64
  113.8 0.0 copy-start.5
  113.9 0.0 reduce-scatter.2.cloned.1.call-update
  113.9 0.0 all-reduce.2.cloned.1.call-start
  114.0 0.8 copy-done
  114.8 0.7 broadcast_select_fusion
  115.5 0.0 all-reduce.2.cloned.1.call-update
  115.5 229.2 %reduce-scatter.2.cloned.1.call-done = f32[16,1792]{1,0:T(8,128)} async-done(((f32[512,1792]{1,0:T(8,128)}), f32[16,1792]{1,0:T(8,128)}) %reduce-scatter.2.cloned.1.call-update) | async-done | bytes 114704 | tf_op jit(solution)/shard_map/reduce_scatter | solution.py:63
  344.8 0.0 copy-done.2
  344.8 0.0 copy-done.4
  344.8 1.6 divide_convert_fusion
  346.4 81.5 %all_gather.14 = bf16[512,896]{1,0:T(8,128)(2,1)S(1)} all-gather(bf16[16,896]{1,0:T(8,128)(2,1)S(1)} %get-tuple-element.14), channel_id=1, replica_groups=mesh['dp'=32,'fsdp'=16] {'dp'}, dimensions={0}, use_global_device_ids=true | all-gather | bytes 946176 | tf_op jit(solution)/shard_map/all_gather | solution.py:75
  427.8 86.6 %all_gather.15 = bf16[512,896]{1,0:T(8,128)(2,1)S(1)} all-gather(bf16[16,896]{1,0:T(8,128)(2,1)S(1)} %get-tuple-element.6), channel_id=1, replica_groups=mesh['dp'=32,'fsdp'=16] {'dp'}, dimensions={0}, use_global_device_ids=true | all-gather | bytes 946176 | tf_op jit(solution)/shard_map/all_gather | solution.py:76
  514.4 2.1 fusion.14
  516.5 0.0 copy-done.1
  516.5 1.1 fusion.12
  (8 shorter events, 0.0 us)
Async XLA Ops:
  7.2 53.8 %all-gather.3.cloned.1.call-start = ((), (), s32[]{:S(2)}) async-start(), calls=%async_computation.2 | async-start | bytes 3342336 | tf_op jit(solution)/shard_map/all_gather | solution.py:46
  7.9 98.1 %all-gather.5.cloned.1.call-start = ((), (), s32[]{:S(2)}) async-start(), calls=%async_computation.3 | async-start | bytes 4456448 | tf_op jit(solution)/shard_map/all_gather | solution.py:49
  8.7 336.1 %reduce-scatter.2.cloned.1.call-start = ((), (), s32[]{:S(2)}) async-start(), calls=%async_computation.4 | async-start | bytes 3784704 | tf_op jit(solution)/shard_map/reduce_scatter | solution.py:63
  113.8 0.9 copy-start
  113.8 230.9 %copy-start.2 = (f32[16,896]{1,0:T(8,128)S(1)}, f32[16,896]{1,0:T(8,128)}, u32[]{:S(2)}) copy-start(f32[16,896]{1,0:T(8,128)} %param.17) | copy-start | bytes 172036
  113.8 230.9 %copy-start.3 = (f32[16,896]{1,0:T(8,128)S(1)}, f32[16,896]{1,0:T(8,128)}, u32[]{:S(2)}) copy-start(f32[16,896]{1,0:T(8,128)} %param.16) | copy-start | bytes 172036
  113.8 230.9 %copy-start.4 = (f32[16,896]{1,0:T(8,128)S(1)}, f32[16,896]{1,0:T(8,128)}, u32[]{:S(2)}) copy-start(f32[16,896]{1,0:T(8,128)} %param.15) | copy-start | bytes 172036
  113.8 230.9 %copy-start.5 = (f32[16,896]{1,0:T(8,128)S(1)}, f32[16,896]{1,0:T(8,128)}, u32[]{:S(2)}) copy-start(f32[16,896]{1,0:T(8,128)} %param.14) | copy-start | bytes 172036
  113.9 400.6 %all-reduce.2.cloned.1.call-start = ((), (), s32[]{:S(2)}) async-start(), calls=%async_computation.1 | async-start | bytes 524288 | tf_op jit(solution)/shard_map/psum | solution.py:9
  514.4 2.1 copy-start.1
Sparse Core Ops, SparseCore 0:
  10.1 50.8 all-gather.2
  63.1 42.8 all-gather.4
  114.0 230.7 reduce-scatter.1
  348.4 124.2 all-reduce.1
where the time goes:
time: 524 us
  waiting for transfers between devices  326 us (62%)
  blocking collectives  168 us (32%)
  between operations  13.8 us (3%)
  matrix products  11 us (2%)
    reduce_scatter x1, waiting for transfers between devices, per_device(): lax.psum_scatter(lax.dot_general(projected, both, (((0,), (0,)), ((), ())...  229 us
    all_gather x1, blocking collectives, per_device(): lax.all_gather(linear_norm, 'dp', axis=0, tiled=True)  86.6 us
    all_gather x1, blocking collectives, per_device(): lax.all_gather(gate_norm, 'dp', axis=0, tiled=True)  81.5 us
    all_gather x1, waiting for transfers between devices, per_device(): features = lax.all_gather(tokens, 'fsdp', axis=1, tiled=True)  50 us
    all_gather x1, waiting for transfers between devices, per_device(): lax.all_gather(basis, 'fsdp', axis=0, tiled=True)  45 us
  transfers between devices with their start and end apart: 4, of which 3 were waited for; matrix products, arithmetic and copies ran while one was open for 1% of the time, Pallas kernels for 0%

commit v1 on v0

v1 whole, which is shorter than its diff:
```python
import functools

import jax
import jax.numpy as jnp
from jax import lax
from jax.experimental import pallas as pl
from jax.experimental.pallas import tpu as pltpu
from jax.sharding import PartitionSpec as P

MESH = pl.DeviceIdType.MESH
Y_PARTS = 4
BF16 = jnp.bfloat16
F32 = jnp.float32


def gradients(logits, values, incoming):
    logits = logits.astype(F32)
    values = values.astype(F32)
    incoming = incoming.astype(F32)
    sig = 1.0 / (1.0 + jnp.exp(-logits))
    gate = incoming * values * sig * (1.0 + logits * (1.0 - sig))
    return gate.astype(BF16), (incoming * (logits * sig)).astype(BF16)


def adam_step(moment, second, grad):
    moment_out = 0.9 * moment + 0.1 * grad
    second_out = 0.999 * second + 0.001 * grad * grad
    normalized = (moment_out / (jnp.sqrt(second_out) + 1e-08)).astype(BF16)
    return moment_out, second_out, normalized


def exchange(
    n_f, n_z, n_h,
    tokens, logits, values, incoming, basis, gate_m, gate_s, lin_m, lin_s,
    norm_out, rows_out, sub_out,
    tok_v, bas_v, log_v, val_v, inc_v, mom_v, sec_v,
    part32, part, a_recv, pt, grad, acc, rs_send, rs_recv, y_send, y_recv, norm, rows_v,
    load_sem, a_ss, a_rs, c_ss, c_rs, b_ss, b_rs, rs_ss, rs_rs, y_ss, y_rs, ya_ss, ya_rs, za_ss, za_rs,
):
    me = lax.axis_index("fsdp")
    dp = lax.axis_index("dp")
    z, h = dp // n_h, dp % n_h
    width = logits.shape[1]
    n_tok = tokens.shape[0]
    rank = basis.shape[1]
    blk = rank // n_f
    chunk = rank // n_z
    half = chunk // 2
    own = chunk // n_h
    n_rows = rows_v.shape[0]

    def z_dev(step):
        return {"dp": ((z + step + n_z) % n_z) * n_h + h}

    def y_dev(k):
        return {"dp": z * n_h + (h + k) % n_h}

    loads = [
        (tokens, tok_v), (basis, bas_v), (logits, log_v), (values, val_v), (incoming, inc_v),
        (gate_m, mom_v.at[0]), (lin_m, mom_v.at[1]), (gate_s, sec_v.at[0]), (lin_s, sec_v.at[1]),
    ]
    loads = [pltpu.make_async_copy(a, b, load_sem.at[i]) for i, (a, b) in enumerate(loads)]
    for c in loads:
        c.start()

    barrier = pltpu.get_barrier_semaphore()
    peers = [{"fsdp": (me + k) % n_f} for k in range(1, n_f)]
    peers += [z_dev(1), z_dev(-1)] + [y_dev(k) for k in range(1, n_h)]
    for p in peers:
        pl.semaphore_signal(barrier, inc=1, device_id=p, device_id_type=MESH)

    loads[0].wait()
    loads[1].wait()
    bt = bas_v[...].T
    part32[...] = lax.dot_general(bt, tok_v[...], (((1,), (1,)), ((), ())), preferred_element_type=F32)
    part[...] = part32[...].astype(BF16)
    pl.semaphore_wait(barrier, len(peers))

    sends = []

    def send(src, dst, ss, rs, dev):
        c = pltpu.make_async_remote_copy(
            src_ref=src, dst_ref=dst, send_sem=ss, recv_sem=rs, device_id=dev, device_id_type=MESH
        )
        c.start()
        sends.append(c)
        return c

    a_copies = []
    for k in range(1, n_f):
        p = (me + k) % n_f
        a_copies.append(
            send(part.at[pl.ds(p * blk, blk)], a_recv.at[k], a_ss.at[k], a_rs.at[k], {"fsdp": p})
        )

    holder = dp * n_rows // bas_v.shape[0]
    local = pl.ds((dp * n_rows) % bas_v.shape[0], n_rows)

    def row_copy(k):
        return pltpu.make_async_remote_copy(
            src_ref=bas_v.at[local], dst_ref=rows_v, send_sem=b_ss.at[k], recv_sem=b_rs,
            device_id={"fsdp": (me + k) % n_f}, device_id_type=MESH,
        )

    @pl.when(me == holder)
    def _():
        for k in range(1, n_f):
            row_copy(k).start()
        rows_v[...] = bas_v[local, :]

    for c in loads[2:5]:
        c.wait()
    step_rows = 32

    def grad_rows(i, _):
        r = pl.ds(pl.multiple_of(i * step_rows, step_rows), step_rows)
        g, l = gradients(log_v[r, :], val_v[r, :], inc_v[r, :])
        grad[r, :width] = g
        grad[r, width:] = l
        return 0

    lax.fori_loop(0, n_tok // step_rows, grad_rows, 0)

    mine = pl.ds(pl.multiple_of(me * blk, blk), blk)
    total = part32[mine, :]
    for k in range(1, n_f):
        a_copies[k - 1].wait_recv()
        total += a_recv[k].astype(F32)
    pt[mine, :] = total.astype(BF16)
    c_copies = [
        send(pt.at[mine], pt.at[mine], c_ss.at[k], c_rs.at[k], {"fsdp": (me + k) % n_f})
        for k in range(1, n_f)
    ]
    for k in range(1, n_f):
        peer = (me + n_f - k) % n_f
        there = pl.ds(pl.multiple_of(peer * blk, blk), blk)
        pltpu.make_async_remote_copy(
            src_ref=pt.at[there], dst_ref=pt.at[there], send_sem=c_ss.at[k], recv_sem=c_rs.at[k],
            device_id={"fsdp": peer}, device_id_type=MESH,
        ).wait_recv()

    def rows_of(t, off=0, size=chunk):
        return pl.ds(pl.multiple_of(((t + n_z) % n_z) * chunk + off, 16), size)

    def cols(c):
        return slice(c * width, (c + 1) * width)

    def product(t, c):
        r = rows_of(t)
        acc[r, cols(c)] = jnp.dot(pt[r, :], grad[:, cols(c)], preferred_element_type=F32)

    hops = n_z // 2
    streams = 2
    ring = {}
    for s in range(hops):
        for c in range(streams):
            for t in sorted({(hops - s) % n_z, (s - hops) % n_z}):
                product(z + t, c)
            for d, sign in ((0, 1), (1, -1)):
                t = z + sign * (hops - s)
                far = slice(0, half) if d == 0 else slice(half, chunk)
                if s == 0:
                    rs_send[c, d, s, far, :] = acc[rows_of(t, d * half, half), cols(c)].astype(BF16)
                    src, dst = rs_send.at[c, d, s, far], rs_recv.at[c, d, s, far]
                else:
                    value = acc[rows_of(t), cols(c)]
                    ring[c, d, s - 1].wait_recv()
                    if s == 1:
                        near = slice(half, chunk) if d == 0 else slice(0, half)
                        rs_send[c, d, s, far, :] = (
                            value[far, :] + rs_recv[c, d, 0, far, :].astype(F32)
                        ).astype(BF16)
                        rs_send[c, d, s, near, :] = value[near, :].astype(BF16)
                    else:
                        rs_send[c, d, s] = (value + rs_recv[c, d, s - 1].astype(F32)).astype(BF16)
                    src, dst = rs_send.at[c, d, s], rs_recv.at[c, d, s]
                ring[c, d, s] = send(src, dst, rs_ss.at[c, d, s], rs_rs.at[c, d, s], z_dev(sign))

    y_copies = {}
    for c in range(streams):
        product(z, c)
        value = acc[rows_of(z), cols(c)]
        for d in range(2):
            ring[c, d, hops - 1].wait_recv()
            value += rs_recv[c, d, hops - 1].astype(F32)
        acc[rows_of(z), cols(c)] = value
        y_send[c] = value.astype(BF16)
        for k in range(1, n_h):
            there = pl.ds(pl.multiple_of(((h + k) % n_h) * own, own), own)
            y_copies[c, k] = send(
                y_send.at[c, there], y_recv.at[c, k], y_ss.at[c, k], y_rs.at[c, k], y_dev(k)
            )

    for c in loads[5:]:
        c.wait()
    my_rows = pl.ds(pl.multiple_of(dp * own, own), own)
    ya = {}
    for c in range(streams):
        value = acc[my_rows, cols(c)]
        for k in range(1, n_h):
            y_copies[c, k].wait_recv()
            value += y_recv[c, k].astype(F32)
        sub_out[:, cols(c)] = value
        norm[my_rows, cols(c)] = adam_step(mom_v[c], sec_v[c], value)[2]
        for k in range(1, n_h):
            piece = norm.at[my_rows, cols(c)]
            ya[c, k] = send(piece, piece, ya_ss.at[c, k], ya_rs.at[c, k], y_dev(k))

    def incoming_copy(piece, ss, rs):
        return pltpu.make_async_remote_copy(
            src_ref=piece, dst_ref=piece, send_sem=ss, recv_sem=rs, device_id=z_dev(1), device_id_type=MESH
        )

    for s in range(hops + 1):
        for c in range(streams):
            if s == 0:
                for k in range(1, n_h):
                    r = pl.ds(pl.multiple_of(z * chunk + ((h + n_h - k) % n_h) * own, own), own)
                    incoming_copy(norm.at[r, cols(c)], ya_ss.at[c, k], ya_rs.at[c, k]).wait_recv()
            for d, sign in ((0, 1), (1, -1)):
                if s > 0:
                    r = rows_of(z - sign * s) if s < hops else rows_of(z - sign * s, d * half, half)
                    incoming_copy(norm.at[r, cols(c)], za_ss.at[c, d, s - 1], za_rs.at[c, d, s - 1]).wait_recv()
                if s < hops:
                    r = rows_of(z - sign * s) if s < hops - 1 else rows_of(z - sign * s, d * half, half)
                    piece = norm.at[r, cols(c)]
                    send(piece, piece, za_ss.at[c, d, s], za_rs.at[c, d, s], z_dev(sign))

    @pl.when(me != holder)
    def _():
        pltpu.make_async_remote_copy(
            src_ref=rows_v, dst_ref=rows_v, send_sem=b_ss.at[0], recv_sem=b_rs,
            device_id={"fsdp": holder}, device_id_type=MESH,
        ).wait_recv()

    @pl.when(me == holder)
    def _():
        for k in range(1, n_f):
            row_copy(k).wait_send()

    norm_out[...] = norm[...]
    rows_out[...] = rows_v[...]
    for c in sends:
        c.wait_send()


def per_device(n_f, n_dp, tokens, logits, values, incoming, basis, gate_m, gate_s, lin_m, lin_s):
    n_h = Y_PARTS
    n_z = n_dp // n_h
    n_tok, depth = tokens.shape
    width = logits.shape[1]
    rank = basis.shape[1]
    own = rank // n_dp
    chunk = rank // n_z
    n_rows = basis.shape[0] * n_f // n_dp
    hops = n_z // 2
    dma = pltpu.SemaphoreType.DMA
    anyspace = pl.BlockSpec(memory_space=pl.ANY)
    vmem = pl.BlockSpec(memory_space=pltpu.VMEM)
    norm, rows, sub = pl.pallas_call(
        functools.partial(exchange, n_f, n_z, n_h),
        out_shape=(
            jax.ShapeDtypeStruct((rank, 2 * width), BF16),
            jax.ShapeDtypeStruct((n_rows, rank), BF16),
            jax.ShapeDtypeStruct((own, 2 * width), F32),
        ),
        in_specs=[anyspace] * 9,
        out_specs=(vmem,) * 3,
        scratch_shapes=[
            pltpu.VMEM((n_tok, depth), BF16),
            pltpu.VMEM(basis.shape, BF16),
            pltpu.VMEM((n_tok, width), BF16),
            pltpu.VMEM((n_tok, width), BF16),
            pltpu.VMEM((n_tok, width), BF16),
            pltpu.VMEM((2, own, width), F32),
            pltpu.VMEM((2, own, width), F32),
            pltpu.VMEM((rank, n_tok), F32),
            pltpu.VMEM((rank, n_tok), BF16),
            pltpu.VMEM((n_f, rank // n_f, n_tok), BF16),
            pltpu.VMEM((rank, n_tok), BF16),
            pltpu.VMEM((n_tok, 2 * width), BF16),
            pltpu.VMEM((rank, 2 * width), F32),
            pltpu.VMEM((2, 2, hops, chunk, width), BF16),
            pltpu.VMEM((2, 2, hops, chunk, width), BF16),
            pltpu.VMEM((2, chunk, width), BF16),
            pltpu.VMEM((2, n_h, own, width), BF16),
            pltpu.VMEM((rank, 2 * width), BF16),
            pltpu.VMEM((n_rows, rank), BF16),
            dma((9,)),
            dma((n_f,)), dma((n_f,)),
            dma((n_f,)), dma((n_f,)),
            dma((n_f,)), dma,
            dma((2, 2, hops)), dma((2, 2, hops)),
            dma((2, n_h)), dma((2, n_h)),
            dma((2, n_h)), dma((2, n_h)),
            dma((2, 2, hops)), dma((2, 2, hops)),
        ],
        compiler_params=pltpu.CompilerParams(
            collective_id=0, has_side_effects=True, vmem_limit_bytes=48 * 1024 * 1024
        ),
    )(tokens, logits, values, incoming, basis, gate_m, gate_s, lin_m, lin_s)
    moment_gate, second_gate, _ = adam_step(gate_m, gate_s, sub[:, :width])
    moment_lin, second_lin, _ = adam_step(lin_m, lin_s, sub[:, width:])
    gate_update = jnp.dot(rows, norm[:, :width], preferred_element_type=F32)
    lin_update = jnp.dot(rows, norm[:, width:], preferred_element_type=F32)
    return gate_update, lin_update, moment_gate, second_gate, moment_lin, second_lin


def solution(mesh):
    both = P("dp", "fsdp")
    return jax.shard_map(
        functools.partial(per_device, mesh.shape["fsdp"], mesh.shape["dp"]),
        mesh=mesh,
        in_specs=(both, both, both, both, P("fsdp", None), both, both, both, both),
        out_specs=(both,) * 6,
        check_vma=False,
    )
```

time: 524 us -> 102 us (0.19)
  the two profiles are of different devices: /device:TPU:16 before, /device:TPU:2 now
where the time goes in v1:
time: 102 us; the launch traced here: 101 us
  Pallas kernels  89.5 us (88%)
  local copies, waits for them, and re-layouts  8.44 us (8%)
  matrix products  2.15 us (2%)
    pallas_call x1, Pallas kernels, per_device(): pl.pallas_call(functools.partial(exchange, n_f, n_z, n_h), out_shape=(jax...  89.5 us
    unnamed x18, local copies, waits for them, and re-layouts  8.44 us

profile of v1, /device:TPU:2, one launch (start us, length us, event | category | flops | bytes accessed | tf_op | source)
XLA Modules:
  0.0 101.5 jit_solution(11704555987305739771)
XLA Ops:
  0.6 0.0 copy-start
  0.6 1.1 %copy-done = bf16[384,896]{1,0:T(8,128)(2,1)S(1)} copy-done((bf16[384,896]{1,0:T(8,128)(2,1)S(1)}, bf16[384,896]{1,0:T(8,128)(2,1)}, u32[]{:S(2)}) %copy-start) | copy-done | bytes 688152
  1.7 0.0 copy-start.1
  1.7 1.1 %copy-done.1 = bf16[384,896]{1,0:T(8,128)(2,1)S(1)} copy-done((bf16[384,896]{1,0:T(8,128)(2,1)S(1)}, bf16[384,896]{1,0:T(8,128)(2,1)}, u32[]{:S(2)}) %copy-start.1) | copy-done | bytes 688152
  2.8 0.0 copy-start.2
  2.8 1.1 %copy-done.2 = bf16[384,896]{1,0:T(8,128)(2,1)S(1)} copy-done((bf16[384,896]{1,0:T(8,128)(2,1)S(1)}, bf16[384,896]{1,0:T(8,128)(2,1)}, u32[]{:S(2)}) %copy-start.2) | copy-done | bytes 688152
  3.9 0.0 copy-start.3
  3.9 0.9 copy-done.3
  4.9 0.0 copy-start.4
  4.9 0.8 copy-done.4
  5.7 0.0 copy-start.5
  5.7 0.8 copy-done.5
  6.5 0.0 copy-start.6
  6.5 0.8 copy-done.6
  7.3 0.0 copy-start.7
  7.3 0.8 copy-done.7
  8.2 0.0 copy-start.8
  8.2 0.9 copy-done.8
  9.1 89.5 %shard_map.136 = (bf16[512,1792]{1,0:T(8,128)(2,1)S(1)}, bf16[128,512]{1,0:T(8,128)(2,1)S(1)}, f32[16,1792]{1,0:T(8,128)S(1)}) custom-call(bf16[384,256]{1,0:T(8,128)(2,1)S(1)} %copy-done.8, bf16[384,896]{1,0:T(8,128)(2,1)S(1)} %copy-done, bf16[384,896]{1,0:T(8,128)(2,1)S(1)} %copy-done.1, bf16[384,896]{1,0:T(8,128)(2,1)S(1)} %copy-done.2, ...), custom_call_target="tpu_custom_call" | custom-call | tf_op jit(solution)/shard_map/pallas_call | solution.py:260
  98.6 1.1 %fusion = f32[128,896]{1,0:T(8,128)} fusion(bf16[128,512]{1,0:T(8,128)(2,1)S(1)} %get-tuple-element.9, bf16[512,1792]{1,0:T(8,128)(2,1)S(1)} %get-tuple-element.10), kind=kOutput, calls=%fused_computation | convolution fusion | flops 117440512 | bytes 1507328 | tf_op jit(solution)/shard_map/dot_general | solution.py:305
  99.7 1.1 %fusion.2 = f32[128,896]{1,0:T(8,128)} fusion(bf16[128,512]{1,0:T(8,128)(2,1)S(1)} %get-tuple-element.9, bf16[512,1792]{1,0:T(8,128)(2,1)S(1)} %get-tuple-element.10), kind=kOutput, calls=%fused_computation.2 | convolution fusion | flops 117440512 | bytes 1507328 | tf_op jit(solution)/shard_map/dot_general | solution.py:304
  100.8 0.7 fusion.5
Async XLA Ops:
  0.6 1.1 %copy-start = (bf16[384,896]{1,0:T(8,128)(2,1)S(1)}, bf16[384,896]{1,0:T(8,128)(2,1)}, u32[]{:S(2)}) copy-start(bf16[384,896]{1,0:T(8,128)(2,1)} %logits.1) | copy-start | bytes 2064388
  1.7 1.1 %copy-start.1 = (bf16[384,896]{1,0:T(8,128)(2,1)S(1)}, bf16[384,896]{1,0:T(8,128)(2,1)}, u32[]{:S(2)}) copy-start(bf16[384,896]{1,0:T(8,128)(2,1)} %values.1) | copy-start | bytes 2064388
  2.8 1.1 %copy-start.2 = (bf16[384,896]{1,0:T(8,128)(2,1)S(1)}, bf16[384,896]{1,0:T(8,128)(2,1)}, u32[]{:S(2)}) copy-start(bf16[384,896]{1,0:T(8,128)(2,1)} %incoming.1) | copy-start | bytes 2064388
  3.9 0.9 copy-start.3
  4.9 0.8 copy-start.4
  5.7 0.8 copy-start.5
  6.5 0.8 copy-start.6
  7.3 0.8 copy-start.7
  8.2 0.9 copy-start.8

commit v2 on v0

v2 whole, which is shorter than its diff:
```python
import functools

import jax
import jax.numpy as jnp
from jax import lax
from jax.experimental import pallas as pl
from jax.experimental.pallas import tpu as pltpu
from jax.sharding import PartitionSpec as P

MESH = pl.DeviceIdType.MESH
Y_PARTS = 4
BF16 = jnp.bfloat16
F32 = jnp.float32
STREAMS = ((0, 512, "z"), (512, 384, "y"), (896, 640, "z"), (1536, 256, "y"))


def gradients(logits, values, incoming):
    logits = logits.astype(F32)
    values = values.astype(F32)
    incoming = incoming.astype(F32)
    sig = 1.0 / (1.0 + jnp.exp(-logits))
    gate = incoming * values * sig * (1.0 + logits * (1.0 - sig))
    return gate.astype(BF16), (incoming * (logits * sig)).astype(BF16)


def exchange(
    n_f, n_z, n_h,
    tokens, logits, values, incoming, basis, gate_m, gate_s, lin_m, lin_s,
    gate_u, lin_u, gate_mo, gate_so, lin_mo, lin_so,
    tok_v, bas_v, bt_v, log_v, val_v, inc_v, mom_v, sec_v,
    part_sib, part_own, core_recv, chip_sum, a_recv, pt, grad, norm, rows_v, upd,
    load_sem, store_sem, ss, rs, b_ss, b_rs, *bufs,
):
    me = lax.axis_index("fsdp")
    dp = lax.axis_index("dp")
    z, h = dp // n_h, dp % n_h
    core, chip = me % 2, me // 2
    n_chip = n_f // 2
    width = logits.shape[1]
    n_tok = tokens.shape[0]
    rank = basis.shape[1]
    own = rank // (n_z * n_h)
    blk = rank // n_f
    n_rows = rows_v.shape[0]
    sibling = {"fsdp": chip * 2 + 1 - core}

    def z_dev(step):
        return {"dp": ((z + step + n_z) % n_z) * n_h + h}

    def y_dev(step):
        return {"dp": z * n_h + (h + step + n_h) % n_h}

    def chip_dev(k):
        return {"fsdp": ((chip + k) % n_chip) * 2 + core}

    gate_c, lin_c = slice(0, width), slice(width, 2 * width)
    loads = [
        (tokens, tok_v), (basis, bas_v), (logits, log_v), (values, val_v), (incoming, inc_v),
        (gate_m, mom_v.at[:, gate_c]), (lin_m, mom_v.at[:, lin_c]),
        (gate_s, sec_v.at[:, gate_c]), (lin_s, sec_v.at[:, lin_c]),
    ]
    loads = [pltpu.make_async_copy(a, b, load_sem.at[i]) for i, (a, b) in enumerate(loads)]
    for c in loads:
        c.start()

    barrier = pltpu.get_barrier_semaphore()
    peers = [sibling] + [chip_dev(k) for k in range(1, n_chip)]
    peers += [z_dev(k) for k in range(1, n_z)] + [y_dev(k) for k in range(1, n_h)]
    for p in peers:
        pl.semaphore_signal(barrier, inc=1, device_id=p, device_id_type=MESH)

    sends = []

    def send(src, dst, dev):
        i = len(sends)
        c = pltpu.make_async_remote_copy(
            src_ref=src, dst_ref=dst, send_sem=ss.at[i], recv_sem=rs.at[i], device_id=dev, device_id_type=MESH
        )
        c.start()
        sends.append(c)
        return c

    loads[1].wait()
    half_rank = rank // 2
    bt_v[...] = bas_v[...].T.reshape(2, half_rank, bas_v.shape[0])
    loads[0].wait()

    def project(which):
        p = lax.dot_general(bt_v[which], tok_v[...], (((1,), (1,)), ((), ())), preferred_element_type=F32)
        return p.reshape(n_chip, blk, n_tok)

    part_sib[...] = project(1 - core)
    pl.semaphore_wait(barrier, len(peers))
    core_copy = send(part_sib, core_recv, sibling)
    part_own[...] = project(core)
    core_copy.wait_recv()
    for q in range(n_chip):
        part_own[q] += core_recv[q]
    chip_sum[...] = part_own[...].astype(BF16)
    a_copies = [send(chip_sum.at[(chip + k) % n_chip], a_recv.at[k], chip_dev(k)) for k in range(1, n_chip)]

    for c in loads[2:5]:
        c.wait()
    step_rows = 32

    def grad_rows(i, _):
        r = pl.ds(pl.multiple_of(i * step_rows, step_rows), step_rows)
        g, l = gradients(log_v[r, :], val_v[r, :], inc_v[r, :])
        grad[r, gate_c] = g
        grad[r, lin_c] = l
        return 0

    lax.fori_loop(0, n_tok // step_rows, grad_rows, 0)

    per = n_h * own // blk
    cuts = blk // own
    block = core * n_chip + chip
    mine = pt.at[block // per, pl.ds((block % per) * cuts, cuts)]
    total = part_own[chip]
    for k in range(1, n_chip):
        a_copies[k - 1].wait_recv()
        total += a_recv[k].astype(F32)
    mine[...] = total.astype(BF16).reshape(cuts, own, n_tok)
    c_copies = [send(mine, mine, chip_dev(k)) for k in range(1, n_chip)]
    for c in c_copies:
        c.wait_recv()
    my_half = pt.at[pl.ds(core * (n_z // 2), n_z // 2)]
    send(my_half, my_half, sibling).wait_recv()

    holder = dp * n_rows // bas_v.shape[0]
    local = pl.ds(pl.multiple_of((dp * n_rows) % bas_v.shape[0], n_rows), n_rows)
    hx, hy, hc = holder // 4, (holder // 2) % 2, holder % 2
    fx, fy = me // 4, (me // 2) % 2
    same_core = core == hc
    is_0 = me == holder
    is_1 = same_core & (fy == hy) & (fx != hx)
    is_2 = same_core & (fy != hy)
    is_3 = core != hc

    def row_copy(i, dev):
        return pltpu.make_async_remote_copy(
            src_ref=rows_v, dst_ref=rows_v, send_sem=b_ss.at[i], recv_sem=b_rs, device_id=dev, device_id_type=MESH
        )

    def down(i):
        return row_copy(i, {"fsdp": (me + 4 * (i + 1)) % n_f})

    to_core = row_copy(n_f // 4, sibling)
    to_y = row_copy(n_f // 4 - 1, {"fsdp": fx * 4 + (1 - fy) * 2 + core})
    n_down = n_f // 4 - 1

    def rows_stream():
        yield 0.1

        @pl.when(is_0)
        def _():
            rows_v[...] = bas_v[local, :]
            for i in range(n_down):
                down(i).start()
            to_y.start()
            to_core.start()

        yield 6.0

        @pl.when(is_1)
        def _():
            to_y.wait_recv()
            to_y.start()
            to_core.start()

        yield 10.0

        @pl.when(is_2)
        def _():
            to_core.wait_recv()
            to_core.start()

        yield 14.0

        @pl.when(is_3)
        def _():
            to_core.wait_recv()

    def columns(first, size):
        return slice(first, first + size)

    def own_step(cs, value):
        moment = 0.9 * mom_v[:, cs] + 0.1 * value
        second = 0.999 * sec_v[:, cs] + 0.001 * value * value
        mom_v[:, cs] = moment
        sec_v[:, cs] = second
        norm[z, h, :, cs] = (moment / (jnp.sqrt(second) + 1e-08)).astype(BF16)

    stores = []

    def expand(first, size):
        cs = columns(first, size)
        upd[:, cs] = jnp.dot(
            rows_v[...], norm[:, :, :, cs].reshape(rank, size), preferred_element_type=F32
        )
        out, at = (gate_u, first) if first < width else (lin_u, first - width)
        c = pltpu.make_async_copy(upd.at[:, cs], out.at[:, at : at + size], store_sem.at[len(stores)])
        c.start()
        stores.append(c)

    def stream(first, size, axis, lag, buf):
        acc, ring_s, ring_r, dir_s, dir_r = buf
        cs = columns(first, size)
        z_first = axis == "z"
        n1, n2 = (n_z, n_h) if z_first else (n_h, n_z)
        p1, p2 = (z, h) if z_first else (h, z)
        dev1, dev2 = (z_dev, y_dev) if z_first else (y_dev, z_dev)
        hops = n1 // 2
        cut = n2 // 2
        far = (slice(0, cut), slice(cut, n2))
        times = (
            ([2, 5, 8, 11, 13, 15, 18, 21, 24, 26] if z_first else [4, 10.5, 13.5, 16.5, 23, 27])
        )
        when = iter([t + lag for t in times])

        def product(slot, t):
            lhs = (pt[t] if z_first else pt[:, t]).reshape(n2 * own, n_tok)
            acc[slot] = jnp.dot(lhs, grad[:, cs], preferred_element_type=F32).reshape(n2, own, size)

        def piece(t, part=slice(0, n2)):
            if z_first:
                return norm.at[t, part, :, cs]
            return norm.at[part, t, :, cs]

        ring = {}
        for s in range(hops):
            for d in range(1 if s == 0 else 2):
                sign = 1 - 2 * d
                product(d, (p1 + sign * (hops - s) + n1) % n1)
            if s > 0:
                yield next(when)
            for d in range(2):
                sign = 1 - 2 * d
                f = far[d]
                if s == 0:
                    ring_s[d, s, f] = acc[0, f].astype(BF16)
                    ring[d, s] = send(ring_s.at[d, s, f], ring_r.at[d, s, f], dev1(sign))
                    continue
                ring[d, s - 1].wait_recv()
                if s == 1:
                    n = far[1 - d]
                    ring_s[d, s, f] = (acc[d, f] + ring_r[d, 0, f].astype(F32)).astype(BF16)
                    ring_s[d, s, n] = acc[d, n].astype(BF16)
                else:
                    ring_s[d, s] = (acc[d] + ring_r[d, s - 1].astype(F32)).astype(BF16)
                ring[d, s] = send(ring_s.at[d, s], ring_r.at[d, s], dev1(sign))
        product(0, p1)
        yield next(when)
        for d in range(2):
            ring[d, hops - 1].wait_recv()
        acc[0] = acc[0] + ring_r[0, hops - 1].astype(F32) + ring_r[1, hops - 1].astype(F32)
        dir_s[...] = acc[0].astype(BF16)
        direct = [send(dir_s.at[(p2 + k) % n2], dir_r.at[k], dev2(k)) for k in range(1, n2)]
        yield next(when)
        value = acc[0, p2]
        for k in range(1, n2):
            direct[k - 1].wait_recv()
            value += dir_r[k].astype(F32)
        own_step(cs, value)
        mine = norm.at[z, h, :, cs]
        direct = [send(mine, mine, dev2(k)) for k in range(1, n2)]
        yield next(when)
        for c in direct:
            c.wait_recv()
        back = {}
        for s in range(hops):
            for d in range(2):
                sign = 1 - 2 * d
                if s > 0:
                    back[d, s - 1].wait_recv()
                t = (p1 - sign * s + n1) % n1
                p = piece(t) if s < hops - 1 else piece(t, far[d])
                back[d, s] = send(p, p, dev1(sign))
            yield next(when)
        for d in range(2):
            back[d, hops - 1].wait_recv()
        expand(first, size)

    for c in loads[5:]:
        c.wait()
    lanes = [stream(f, w, axis, i * 0.5, bufs[5 * i : 5 * i + 5]) for i, (f, w, axis) in enumerate(STREAMS)]
    lanes.append(rows_stream())
    queue = [(next(g), i, g) for i, g in enumerate(lanes)]
    while queue:
        queue.sort(key=lambda e: e[:2])
        _, i, g = queue.pop(0)
        t = next(g, None)
        if t is not None:
            queue.append((t, i, g))

    outs = [
        (mom_v.at[:, gate_c], gate_mo), (sec_v.at[:, gate_c], gate_so),
        (mom_v.at[:, lin_c], lin_mo), (sec_v.at[:, lin_c], lin_so),
    ]
    for a, b in outs:
        c = pltpu.make_async_copy(a, b, store_sem.at[len(stores)])
        c.start()
        stores.append(c)

    @pl.when(is_0)
    def _():
        for i in range(n_down):
            down(i).wait_send()

    @pl.when(is_0 | is_1)
    def _():
        to_y.wait_send()

    @pl.when(same_core)
    def _():
        to_core.wait_send()

    for c in sends:
        c.wait_send()
    for c in stores:
        c.wait()


def copy_out(n, *refs):
    stage, sem = refs[2 * n : 3 * n], refs[-1]
    reads = [pltpu.make_async_copy(refs[i], stage[i], sem.at[i]) for i in range(n)]
    writes = [pltpu.make_async_copy(stage[i], refs[n + i], sem.at[n + i]) for i in range(n)]
    for c in reads:
        c.start()
    for r, w in zip(reads, writes):
        r.wait()
        w.start()
    for c in writes:
        c.wait()


def per_device(n_f, n_dp, tokens, logits, values, incoming, basis, gate_m, gate_s, lin_m, lin_s):
    n_h = Y_PARTS
    n_z = n_dp // n_h
    n_tok, depth = tokens.shape
    width = logits.shape[1]
    rank = basis.shape[1]
    own = rank // n_dp
    n_rows = basis.shape[0] * n_f // n_dp
    blk = rank // n_f
    dma = pltpu.SemaphoreType.DMA
    hbm = pl.BlockSpec(memory_space=pltpu.HBM)
    bufs = []
    for _, size, axis in STREAMS:
        n1, n2 = (n_z, n_h) if axis == "z" else (n_h, n_z)
        bufs += [
            pltpu.VMEM((2, n2, own, size), F32),
            pltpu.VMEM((2, n1 // 2, n2, own, size), BF16),
            pltpu.VMEM((2, n1 // 2, n2, own, size), BF16),
            pltpu.VMEM((n2, own, size), BF16),
            pltpu.VMEM((n2, own, size), BF16),
        ]
    outs = tuple(
        jax.ShapeDtypeStruct((r, width), F32) for r in (n_rows, n_rows, own, own, own, own)
    )
    done = pl.pallas_call(
        functools.partial(exchange, n_f, n_z, n_h),
        out_shape=outs,
        in_specs=[hbm] * 9,
        out_specs=(hbm,) * 6,
        scratch_shapes=[
            pltpu.VMEM((n_tok, depth), BF16),
            pltpu.VMEM(basis.shape, BF16),
            pltpu.VMEM((2, rank // 2, depth), BF16),
            pltpu.VMEM((n_tok, width), BF16),
            pltpu.VMEM((n_tok, width), BF16),
            pltpu.VMEM((n_tok, width), BF16),
            pltpu.VMEM((own, 2 * width), F32),
            pltpu.VMEM((own, 2 * width), F32),
            pltpu.VMEM((n_f // 2, blk, n_tok), F32),
            pltpu.VMEM((n_f // 2, blk, n_tok), F32),
            pltpu.VMEM((n_f // 2, blk, n_tok), F32),
            pltpu.VMEM((n_f // 2, blk, n_tok), BF16),
            pltpu.VMEM((n_f // 2, blk, n_tok), BF16),
            pltpu.VMEM((n_z, n_h, own, n_tok), BF16),
            pltpu.VMEM((n_tok, 2 * width), BF16),
            pltpu.VMEM((n_z, n_h, own, 2 * width), BF16),
            pltpu.VMEM((n_rows, rank), BF16),
            pltpu.VMEM((n_rows, 2 * width), F32),
            dma((9,)),
            dma((len(STREAMS) + 4,)),
            dma((128,)),
            dma((128,)),
            dma((n_f // 4 + 1,)),
            dma,
            *bufs,
        ],
        compiler_params=pltpu.CompilerParams(
            collective_id=0, has_side_effects=True, vmem_limit_bytes=64 * 1024 * 1024
        ),
    )(tokens, logits, values, incoming, basis, gate_m, gate_s, lin_m, lin_s)
    gate_u, lin_u, mg, sg, ml, sl = pl.pallas_call(
        functools.partial(copy_out, 6),
        out_shape=outs,
        in_specs=[hbm] * 6,
        out_specs=(hbm,) * 6,
        scratch_shapes=[pltpu.VMEM(o.shape, F32) for o in outs] + [dma((12,))],
    )(*done)
    return gate_u, lin_u, mg, sg, ml, sl


def solution(mesh):
    both = P("dp", "fsdp")
    return jax.shard_map(
        functools.partial(per_device, mesh.shape["fsdp"], mesh.shape["dp"]),
        mesh=mesh,
        in_specs=(both, both, both, both, P("fsdp", None), both, both, both, both),
        out_specs=(both,) * 6,
        check_vma=False,
    )
```

time: 524 us -> 77.1 us (0.15)
  the two profiles are of different devices: /device:TPU:16 before, /device:TPU:64 now
where the time goes in v2:
time: 77.1 us; the launch traced here: 76.9 us
  Pallas kernels  76.3 us (99%)
    pallas_call x1, Pallas kernels, per_device(): pl.pallas_call(functools.partial(exchange, n_f, n_z, n_h), out_shape=outs...  74.2 us
    pallas_call x1, Pallas kernels, per_device(): pl.pallas_call(functools.partial(copy_out, 6), out_shape=outs, in_specs=[...  2.11 us

profile of v2, /device:TPU:64, one launch (start us, length us, event | category | flops | bytes accessed | tf_op | source)
XLA Modules:
  0.0 76.9 jit_solution(16725180613807479176)
XLA Ops:
  0.6 74.2 %shard_map.136 = (f32[128,896]{1,0:T(8,128)}, f32[128,896]{1,0:T(8,128)}, f32[16,896]{1,0:T(8,128)}, f32[16,896]{1,0:T(8,128)}, f32[16,896]{1,0:T(8,128)}, /*index=5*/f32[16,896]{1,0:T(8,128)}) custom-call(bf16[384,256]{1,0:T(8,128)(2,1)} %tokens.1, bf16[384,896]{1,0:T(8,128)(2,1)} %logits.1, bf16[384,896]{1,0:T(8,128)(2,1)} %values.1, ...), custom_call_target="tpu_custom_call" | custom-call | tf_op jit(solution)/shard_map/pallas_call | solution.py:361
  74.8 2.1 %shard_map.137 = (f32[128,896]{1,0:T(8,128)}, f32[128,896]{1,0:T(8,128)}, f32[16,896]{1,0:T(8,128)}, f32[16,896]{1,0:T(8,128)}, f32[16,896]{1,0:T(8,128)}, /*index=5*/f32[16,896]{1,0:T(8,128)}) custom-call(f32[128,896]{1,0:T(8,128)} %get-tuple-element.12.refs_0_, f32[128,896]{1,0:T(8,128)} %get-tuple-element.13.refs_1_, ...), custom_call_target="tpu_custom_call" | custom-call | tf_op jit(solution)/shard_map/pallas_call | solution.py:397

commit v3 on v2

--- a/solution.py
+++ b/solution.py
@@ -11,7 +11,7 @@
 Y_PARTS = 4
 BF16 = jnp.bfloat16
 F32 = jnp.float32
-STREAMS = ((0, 512, "z"), (512, 384, "y"), (896, 640, "z"), (1536, 256, "y"))
+STREAMS = ((0, 384, 'z'), (384, 384, 'y'), (768, 384, 'z'), (1152, 256, 'y'), (1408, 384, 'z'))
 
 
 def gradients(logits, values, incoming):
@@ -184,24 +184,35 @@
     def columns(first, size):
         return slice(first, first + size)
 
+    stores, stepped = [], []
+
+    def store(src, dst):
+        c = pltpu.make_async_copy(src, dst, store_sem.at[len(stores)])
+        c.start()
+        stores.append(c)
+
     def own_step(cs, value):
         moment = 0.9 * mom_v[:, cs] + 0.1 * value
         second = 0.999 * sec_v[:, cs] + 0.001 * value * value
         mom_v[:, cs] = moment
         sec_v[:, cs] = second
         norm[z, h, :, cs] = (moment / (jnp.sqrt(second) + 1e-08)).astype(BF16)
-
-    stores = []
+        stepped.append(cs)
+        if len(stepped) == len(STREAMS):
+            store(mom_v.at[:, gate_c], gate_mo)
+            store(sec_v.at[:, gate_c], gate_so)
+            store(mom_v.at[:, lin_c], lin_mo)
+            store(sec_v.at[:, lin_c], lin_so)
 
     def expand(first, size):
         cs = columns(first, size)
         upd[:, cs] = jnp.dot(
             rows_v[...], norm[:, :, :, cs].reshape(rank, size), preferred_element_type=F32
         )
-        out, at = (gate_u, first) if first < width else (lin_u, first - width)
-        c = pltpu.make_async_copy(upd.at[:, cs], out.at[:, at : at + size], store_sem.at[len(stores)])
-        c.start()
-        stores.append(c)
+        for out, low in ((gate_u, 0), (lin_u, width)):
+            begin, end = max(first, low), min(first + size, low + width)
+            if begin < end:
+                store(upd.at[:, begin:end], out.at[:, begin - low : end - low])
 
     def stream(first, size, axis, lag, buf):
         acc, ring_s, ring_r, dir_s, dir_r = buf
@@ -214,7 +225,7 @@
         cut = n2 // 2
         far = (slice(0, cut), slice(cut, n2))
         times = (
-            ([2, 5, 8, 11, 13, 15, 18, 21, 24, 26] if z_first else [4, 10.5, 13.5, 16.5, 23, 27])
+            ([2, 5, 8, 11, 13, 15, 18, 21, 24, 26] if z_first else [3, 9.5, 12.5, 15.5, 22, 26])
         )
         when = iter([t + lag for t in times])
 
@@ -283,8 +294,18 @@
 
     for c in loads[5:]:
         c.wait()
-    lanes = [stream(f, w, axis, i * 0.5, bufs[5 * i : 5 * i + 5]) for i, (f, w, axis) in enumerate(STREAMS)]
+    lanes = [stream(f, w, axis, i * 0.3, bufs[5 * i : 5 * i + 5]) for i, (f, w, axis) in enumerate(STREAMS)]
     lanes.append(rows_stream())
+    marks, settled = [], [0]
+
+    def settle():
+        marks.append(len(sends))
+        if len(marks) > 2 * len(lanes):
+            upto = marks[-2 * len(lanes) - 1]
+            for c in sends[settled[0] : upto]:
+                c.wait_send()
+            settled[0] = upto
+
     queue = [(next(g), i, g) for i, g in enumerate(lanes)]
     while queue:
         queue.sort(key=lambda e: e[:2])
@@ -292,15 +313,7 @@
         t = next(g, None)
         if t is not None:
             queue.append((t, i, g))
-
-    outs = [
-        (mom_v.at[:, gate_c], gate_mo), (sec_v.at[:, gate_c], gate_so),
-        (mom_v.at[:, lin_c], lin_mo), (sec_v.at[:, lin_c], lin_so),
-    ]
-    for a, b in outs:
-        c = pltpu.make_async_copy(a, b, store_sem.at[len(stores)])
-        c.start()
-        stores.append(c)
+        settle()
 
     @pl.when(is_0)
     def _():
@@ -315,7 +328,7 @@
     def _():
         to_core.wait_send()
 
-    for c in sends:
+    for c in sends[settled[0] :]:
         c.wait_send()
     for c in stores:
         c.wait()
@@ -346,8 +359,10 @@
     dma = pltpu.SemaphoreType.DMA
     hbm = pl.BlockSpec(memory_space=pltpu.HBM)
     bufs = []
+    n_sends = n_f
     for _, size, axis in STREAMS:
         n1, n2 = (n_z, n_h) if axis == "z" else (n_h, n_z)
+        n_sends += 2 * n1 + 2 * (n2 - 1)
         bufs += [
             pltpu.VMEM((2, n2, own, size), F32),
             pltpu.VMEM((2, n1 // 2, n2, own, size), BF16),
@@ -383,9 +398,9 @@
             pltpu.VMEM((n_rows, rank), BF16),
             pltpu.VMEM((n_rows, 2 * width), F32),
             dma((9,)),
-            dma((len(STREAMS) + 4,)),
-            dma((128,)),
-            dma((128,)),
+            dma((len(STREAMS) + 5,)),
+            dma((n_sends,)),
+            dma((n_sends,)),
             dma((n_f // 4 + 1,)),
             dma,
             *bufs,

time: 77.1 us -> 74.9 us (0.971)
  the two profiles are of different devices: /device:TPU:64 before, /device:TPU:2 now
where the time goes in v3:
time: 74.9 us; the launch traced here: 74.7 us
  Pallas kernels  74.1 us (99%)
    pallas_call x1, Pallas kernels, per_device(): pl.pallas_call(functools.partial(exchange, n_f, n_z, n_h), out_shape=outs...  71.9 us
    pallas_call x1, Pallas kernels, per_device(): pl.pallas_call(functools.partial(copy_out, 6), out_shape=outs, in_specs=[...  2.11 us

profile of v3, /device:TPU:2, one launch (start us, length us, event | category | flops | bytes accessed | tf_op | source)
XLA Modules:
  0.0 74.7 jit_solution(11332622506346123299)
XLA Ops:
  0.6 71.9 %shard_map.136 = (f32[128,896]{1,0:T(8,128)}, f32[128,896]{1,0:T(8,128)}, f32[16,896]{1,0:T(8,128)}, f32[16,896]{1,0:T(8,128)}, f32[16,896]{1,0:T(8,128)}, /*index=5*/f32[16,896]{1,0:T(8,128)}) custom-call(bf16[384,256]{1,0:T(8,128)(2,1)} %tokens.1, bf16[384,896]{1,0:T(8,128)(2,1)} %logits.1, bf16[384,896]{1,0:T(8,128)(2,1)} %values.1, ...), custom_call_target="tpu_custom_call" | custom-call | tf_op jit(solution)/shard_map/pallas_call | solution.py:376
  72.6 2.1 %shard_map.137 = (f32[128,896]{1,0:T(8,128)}, f32[128,896]{1,0:T(8,128)}, f32[16,896]{1,0:T(8,128)}, f32[16,896]{1,0:T(8,128)}, f32[16,896]{1,0:T(8,128)}, /*index=5*/f32[16,896]{1,0:T(8,128)}) custom-call(f32[128,896]{1,0:T(8,128)} %get-tuple-element.12.refs_0_, f32[128,896]{1,0:T(8,128)} %get-tuple-element.13.refs_1_, ...), custom_call_target="tpu_custom_call" | custom-call | tf_op jit(solution)/shard_map/pallas_call | solution.py:412

commit v4 on v3

--- a/solution.py
+++ b/solution.py
@@ -71,14 +71,31 @@
 
     sends = []
 
+    used = [0]
+
     def send(src, dst, dev):
-        i = len(sends)
+        i = used[0]
+        used[0] += 1
         c = pltpu.make_async_remote_copy(
             src_ref=src, dst_ref=dst, send_sem=ss.at[i], recv_sem=rs.at[i], device_id=dev, device_id_type=MESH
         )
         c.start()
         sends.append(c)
         return c
+
+    def send_all(pairs, landing):
+        i = used[0]
+        used[0] += 1
+        for src, dst, dev in pairs:
+            pltpu.make_async_remote_copy(
+                src_ref=src, dst_ref=dst, send_sem=ss.at[i], recv_sem=rs.at[i], device_id=dev, device_id_type=MESH
+            ).start()
+        whole = pltpu.make_async_remote_copy(
+            src_ref=landing, dst_ref=landing, send_sem=ss.at[i], recv_sem=rs.at[i],
+            device_id=sibling, device_id_type=MESH,
+        )
+        sends.append(whole)
+        return whole
 
     loads[1].wait()
     half_rank = rank // 2
@@ -97,7 +114,10 @@
     for q in range(n_chip):
         part_own[q] += core_recv[q]
     chip_sum[...] = part_own[...].astype(BF16)
-    a_copies = [send(chip_sum.at[(chip + k) % n_chip], a_recv.at[k], chip_dev(k)) for k in range(1, n_chip)]
+    others = range(1, n_chip)
+    a_copy = send_all(
+        [(chip_sum.at[(chip + k) % n_chip], a_recv.at[k], chip_dev(k)) for k in others], a_recv.at[1:]
+    )
 
     for c in loads[2:5]:
         c.wait()
@@ -117,13 +137,11 @@
     block = core * n_chip + chip
     mine = pt.at[block // per, pl.ds((block % per) * cuts, cuts)]
     total = part_own[chip]
-    for k in range(1, n_chip):
-        a_copies[k - 1].wait_recv()
+    a_copy.wait_recv()
+    for k in others:
         total += a_recv[k].astype(F32)
     mine[...] = total.astype(BF16).reshape(cuts, own, n_tok)
-    c_copies = [send(mine, mine, chip_dev(k)) for k in range(1, n_chip)]
-    for c in c_copies:
-        c.wait_recv()
+    send_all([(mine, mine, chip_dev(k)) for k in others], a_recv.at[1:]).wait_recv()
     my_half = pt.at[pl.ds(core * (n_z // 2), n_z // 2)]
     send(my_half, my_half, sibling).wait_recv()
 
@@ -266,18 +284,19 @@
             ring[d, hops - 1].wait_recv()
         acc[0] = acc[0] + ring_r[0, hops - 1].astype(F32) + ring_r[1, hops - 1].astype(F32)
         dir_s[...] = acc[0].astype(BF16)
-        direct = [send(dir_s.at[(p2 + k) % n2], dir_r.at[k], dev2(k)) for k in range(1, n2)]
+        direct = send_all(
+            [(dir_s.at[(p2 + k) % n2], dir_r.at[k], dev2(k)) for k in range(1, n2)], dir_r.at[1:]
+        )
         yield next(when)
         value = acc[0, p2]
+        direct.wait_recv()
         for k in range(1, n2):
-            direct[k - 1].wait_recv()
             value += dir_r[k].astype(F32)
         own_step(cs, value)
         mine = norm.at[z, h, :, cs]
-        direct = [send(mine, mine, dev2(k)) for k in range(1, n2)]
+        direct = send_all([(mine, mine, dev2(k)) for k in range(1, n2)], dir_r.at[1:])
         yield next(when)
-        for c in direct:
-            c.wait_recv()
+        direct.wait_recv()
         back = {}
         for s in range(hops):
             for d in range(2):
@@ -359,10 +378,10 @@
     dma = pltpu.SemaphoreType.DMA
     hbm = pl.BlockSpec(memory_space=pltpu.HBM)
     bufs = []
-    n_sends = n_f
+    n_sends = 4
     for _, size, axis in STREAMS:
         n1, n2 = (n_z, n_h) if axis == "z" else (n_h, n_z)
-        n_sends += 2 * n1 + 2 * (n2 - 1)
+        n_sends += 2 * n1 + 2
         bufs += [
             pltpu.VMEM((2, n2, own, size), F32),
             pltpu.VMEM((2, n1 // 2, n2, own, size), BF16),

time: 74.9 us -> 73.9 us (0.987)
  Pallas kernels: 74.1 us -> 73.1 us
    pallas_call x1, Pallas kernels: 71.9 us -> 71 us  [per_device(): pl.pallas_call(functools.partial(exchange, n_f, n_z, n_h), out_shape=outs...]
where the time goes in v4:
time: 73.9 us; the launch traced here: 73.7 us
  Pallas kernels  73.1 us (99%)
    pallas_call x1, Pallas kernels, per_device(): pl.pallas_call(functools.partial(exchange, n_f, n_z, n_h), out_shape=outs...  71 us
    pallas_call x1, Pallas kernels, per_device(): pl.pallas_call(functools.partial(copy_out, 6), out_shape=outs, in_specs=[...  2.11 us

profile of v4, /device:TPU:2, one launch (start us, length us, event | category | flops | bytes accessed | tf_op | source)
XLA Modules:
  0.0 73.7 jit_solution(2770740959247424882)
XLA Ops:
  0.6 71.0 %shard_map.136 = (f32[128,896]{1,0:T(8,128)}, f32[128,896]{1,0:T(8,128)}, f32[16,896]{1,0:T(8,128)}, f32[16,896]{1,0:T(8,128)}, f32[16,896]{1,0:T(8,128)}, /*index=5*/f32[16,896]{1,0:T(8,128)}) custom-call(bf16[384,256]{1,0:T(8,128)(2,1)} %tokens.1, bf16[384,896]{1,0:T(8,128)(2,1)} %logits.1, bf16[384,896]{1,0:T(8,128)(2,1)} %values.1, ...), custom_call_target="tpu_custom_call" | custom-call | tf_op jit(solution)/shard_map/pallas_call | solution.py:395
  71.6 2.1 %shard_map.137 = (f32[128,896]{1,0:T(8,128)}, f32[128,896]{1,0:T(8,128)}, f32[16,896]{1,0:T(8,128)}, f32[16,896]{1,0:T(8,128)}, f32[16,896]{1,0:T(8,128)}, /*index=5*/f32[16,896]{1,0:T(8,128)}) custom-call(f32[128,896]{1,0:T(8,128)} %get-tuple-element.12.refs_0_, f32[128,896]{1,0:T(8,128)} %get-tuple-element.13.refs_1_, ...), custom_call_target="tpu_custom_call" | custom-call | tf_op jit(solution)/shard_map/pallas_call | solution.py:431
